TPU v7x, 32 devices: a whole 2x2x4 slice. The times are simulated.
32 devices in a mesh: section: 2 (over x), tok: 16 (over z, y, core).
Axes of the slice: x: 2, y: 2, z: 4, core: 2. Of those that a mesh axis runs over, the one named last changes fastest.
Arguments:
- queries: bfloat16 [2, 4096, 4096], P('section', 'tok'), may hold values from -120 to 120
- suffix_kv: bfloat16 [2, 4096, 1024], P('section', 'tok'), may hold values from -4 to 4
- prefix_kv: bfloat16 [2, 16, 64, 1024], P('section', 'tok'), may hold values from -4 to 4
- served: int32 [2, 32, 8], P('section'), may hold values from -1 to 15, as said below
Outputs:
- passed: bfloat16 [2, 4096, 4096], P('section', 'tok')
Inputs may be any that keep to these rules, and one draw needn't show every extreme that they name: `served`: entry k of a row is -1 or a page in [k * 2, (k + 1) * 2); live entries come first, then -1; entry 0 is always live, and block 0 of every section has all 8 live.
All inputs are finite; a program needn't handle non-finite values.
Results may differ from a plain program's by a relative error of at most 0.0029.
Values may be sent and summed in bfloat16 or wider, within the bound.
A program may use at most 64 MiB of HBM per device.

v0:
```python
import math

import jax
import jax.numpy as jnp
from jax import lax
from jax.sharding import PartitionSpec as P

Q_HEADS = 32
KV_HEADS = 4
HEAD = 128
BLOCK = 128
PAGE = 64
QB_DEV = 2
DEPTH = 8


def from_behind(x, axis, by):
    devices = lax.axis_size(axis)
    return lax.ppermute(x, axis, [(i, (i + by) % devices) for i in range(devices)])


def attend(query_rows, key_rows, value_rows, allowed, score_scale):
    scores = (
        jnp.einsum("qgd,kd->gqk", query_rows, key_rows, preferred_element_type=jnp.float32)
        * score_scale
    )
    scores = jnp.where(allowed[None], scores, -jnp.inf)
    row_top = jnp.max(scores, axis=2, keepdims=True)
    exponent = jnp.exp(scores - row_top)
    totals = jnp.sum(exponent, axis=2)
    weights = exponent.astype(jnp.bfloat16)
    mixture = jnp.einsum("gqk,kd->qgd", weights, value_rows, preferred_element_type=jnp.float32)
    return (mixture / jnp.transpose(totals)[:, :, None]).astype(jnp.bfloat16)


def on_device(queries, suffix_kv, prefix_kv, served):
    tok_count = lax.axis_size("tok")
    my_index = lax.axis_index("tok")
    group_size = Q_HEADS // KV_HEADS
    score_scale = 1.0 / math.sqrt(HEAD)
    first_block = my_index * QB_DEV
    my_served = lax.dynamic_slice_in_dim(served[0], first_block, QB_DEV, 0)
    readers = jnp.any(served[0].reshape(tok_count, QB_DEV * DEPTH) == my_index, axis=1)
    own_page = prefix_kv[0, 0]
    outgoing = jnp.where(readers[:, None, None], own_page[None], jnp.zeros_like(own_page)[None])
    arrived = lax.all_to_all(outgoing, "tok", split_axis=0, concat_axis=0, tiled=True)
    chosen = arrived[jnp.maximum(my_served, 0)]
    prefix_pairs = chosen.reshape(QB_DEV, DEPTH * PAGE, 2, KV_HEADS, HEAD)
    own_pairs = suffix_kv[0].reshape(QB_DEV, BLOCK, 2, KV_HEADS, HEAD)
    query_blocks = queries[0].reshape(QB_DEV, BLOCK, KV_HEADS, group_size, HEAD)
    live_rows = jnp.broadcast_to((my_served >= 0)[:, :, None], (QB_DEV, DEPTH, PAGE))
    live_rows = live_rows.reshape(QB_DEV, DEPTH * PAGE)
    row_index = lax.broadcasted_iota(jnp.int32, (BLOCK, BLOCK), 0)
    col_index = lax.broadcasted_iota(jnp.int32, (BLOCK, BLOCK), 1)
    causal = col_index <= row_index

    def per_item(position):
        block_id = position // KV_HEADS
        head_id = position % KV_HEADS
        key_rows = jnp.concatenate(
            [prefix_pairs[block_id, :, 0, head_id], own_pairs[block_id, :, 0, head_id]], axis=0
        )
        value_rows = jnp.concatenate(
            [prefix_pairs[block_id, :, 1, head_id], own_pairs[block_id, :, 1, head_id]], axis=0
        )
        allowed = jnp.concatenate(
            [jnp.broadcast_to(live_rows[block_id][None], (BLOCK, DEPTH * PAGE)), causal], axis=1
        )
        return attend(
            query_blocks[block_id, :, head_id], key_rows, value_rows, allowed, score_scale
        )

    results = lax.map(per_item, jnp.arange(QB_DEV * KV_HEADS))
    results = results.reshape(QB_DEV, KV_HEADS, BLOCK, group_size * HEAD)
    attention = jnp.transpose(results, (0, 2, 1, 3)).reshape(1, QB_DEV * BLOCK, Q_HEADS * HEAD)
    return from_behind(attention, "section", 1)


def solution(mesh):
    placed = (
        P("section", "tok", None),
        P("section", "tok", None),
        P("section", "tok", None, None),
        P("section", None, None),
    )
    return jax.shard_map(
        on_device, mesh=mesh, in_specs=placed, out_specs=P("section", "tok", None), check_vma=False
    )
```

profile of v0, /device:TPU:12, one launch (start us, length us, event | category | flops | bytes accessed | tf_op | source)
XLA Modules:
  0.0 184.1 jit_solution(3549066146431623301)
XLA Ops:
  0.0 0.7 compare_reduce_fusion
  0.9 2.4 %broadcast_select_fusion = bf16[16,64,1024]{2,1,0:T(8,128)(2,1)} fusion(pred[16]{0:T(512)(128)(4,1)S(1)} %reduce_or.18, bf16[64,1024]{1,0:T(8,128)(2,1)} %bitcast.92), kind=kLoop, calls=%fused_computation.34 | loop fusion | flops 1048576 | bytes 2228240 | tf_op jit(solution)/shard_map/jit(_where)/select_n | solution.py:45
  3.3 6.4 %all-to-all-start = ((bf16[16,64,1024]{2,1,0:T(8,128)(2,1)}), bf16[16,64,1024]{2,1,0:T(8,128)(2,1)S(1)}, u32[]{:S(2)}, u32[]{:S(2)}) async-start(bf16[16,64,1024]{2,1,0:T(8,128)(2,1)} %broadcast_select_fusion), calls=%async_computation | async-start | bytes 4194304 | tf_op jit(solution)/shard_map/all_to_all | solution.py:46
  10.3 3.5 %copy.22 = bf16[32,8,32,128]{3,2,1,0:T(8,128)(2,1)} copy(bf16[32,8,32,128]{3,1,2,0:T(8,128)(2,1)} %bitcast.89) | data formatting | bytes 4194304
  14.3 42.7 %all-to-all-done = bf16[16,64,1024]{2,1,0:T(8,128)(2,1)S(1)} async-done(((bf16[16,64,1024]{2,1,0:T(8,128)(2,1)}), bf16[16,64,1024]{2,1,0:T(8,128)(2,1)S(1)}, u32[]{:S(2)}, u32[]{:S(2)}) %all-to-all-start) | async-done | bytes 2097184 | tf_op jit(solution)/shard_map/all_to_all | solution.py:46
  57.0 2.0 %gather_fusion = bf16[16,64,1024]{2,1,0:T(8,128)(2,1)} fusion(bf16[16,64,1024]{2,1,0:T(8,128)(2,1)S(1)} %all-to-all-done, s32[1024]{0:T(1024)S(1)} %pad_clamp_fusion), kind=kCustom, calls=%fused_computation | custom fusion | bytes 4194368 | tf_op jit(solution)/shard_map/gather | solution.py:47
  59.0 3.2 %reshape.38 = bf16[2,512,2,4,128]{4,3,2,1,0:T(4,128)(2,1)S(1)} reshape(bf16[16,64,1024]{2,1,0:T(8,128)(2,1)} %gather_fusion) | data formatting | bytes 4194304 | tf_op jit(solution)/shard_map/reshape | solution.py:48
  62.2 1.6 copy.16
  63.8 64.7 %while.13 = (s32[]{:T(128)}, bf16[8,128,8,128]{1,3,2,0:T(8,128)(2,1)}, s32[8]{0:T(128)S(1)}, bf16[2,512,2,4,128]{4,1,3,2,0:T(8,128)(2,1)}, bf16[2,128,2,4,128]{4...) while((s32[]{:T(128)}, ...), condition=%wide.region_5.6_spmd.clone, body=%wide.region_2.5_spmd.clone.sunk | while | flops 343767072 | bytes 10608301 | solution.py:73
  63.8 0.6 dynamic_slice.71
  66.9 1.0 constant_dynamic-slice_fusion.8
  67.9 1.0 constant_dynamic-slice_fusion.6
  69.6 0.5 fusion.38
  70.4 1.5 fusion.39
  71.9 0.6 dynamic_slice.71
  75.0 1.0 constant_dynamic-slice_fusion.8
  76.0 1.0 constant_dynamic-slice_fusion.6
  77.7 0.5 fusion.38
  78.5 1.5 fusion.39
  80.0 0.6 dynamic_slice.71
  83.1 1.0 constant_dynamic-slice_fusion.8
  84.1 1.0 constant_dynamic-slice_fusion.6
  86.6 1.5 fusion.39
  88.1 0.6 dynamic_slice.71
  91.2 1.0 constant_dynamic-slice_fusion.8
  92.2 1.0 constant_dynamic-slice_fusion.6
  94.7 1.5 fusion.39
  96.2 0.6 dynamic_slice.71
  99.3 1.0 constant_dynamic-slice_fusion.8
  100.3 1.0 constant_dynamic-slice_fusion.6
  102.8 1.5 fusion.39
  104.3 0.6 dynamic_slice.71
  107.4 1.0 constant_dynamic-slice_fusion.8
  108.4 1.0 constant_dynamic-slice_fusion.6
  110.9 1.5 fusion.39
  112.4 0.6 dynamic_slice.71
  115.5 1.0 constant_dynamic-slice_fusion.8
  116.5 1.0 constant_dynamic-slice_fusion.6
  119.0 1.5 fusion.39
  120.5 0.6 dynamic_slice.71
  123.6 1.0 constant_dynamic-slice_fusion.8
  124.6 1.0 constant_dynamic-slice_fusion.6
  127.1 1.5 fusion.39
  128.6 3.4 %copy.19 = bf16[2,4,128,1024]{3,1,2,0:T(4,128)(2,1)S(1)} copy(bf16[2,4,128,1024]{2,3,1,0:T(8,128)(2,1)} %bitcast.90) | data formatting | bytes 4194304 | tf_op jit(solution)/shard_map/reshape | solution.py:74
  131.9 2.8 %reshape.41 = bf16[1,256,4096]{2,1,0:T(8,128)(2,1)} reshape(bf16[2,128,4,1024]{3,2,1,0:T(4,128)(2,1)S(1)} %bitcast.86) | data formatting | bytes 4194304 | tf_op jit(solution)/shard_map/reshape | solution.py:75
  134.7 1.5 collective-permute-start
  136.2 46.5 %collective-permute-done = bf16[1,256,4096]{2,1,0:T(8,128)(2,1)S(1)} collective-permute-done((bf16[1,256,4096]{2,1,0:T(8,128)(2,1)}, bf16[1,256,4096]{2,1,0:T(8,128)(2,1)S(1)}, u32[]{:S(2)}, u32[]{:S(2)}) %collective-permute-start) | collective-permute-done | bytes 2097184 | tf_op jit(solution)/shard_map/ppermute | solution.py:19
  182.8 1.3 copy.41
  (88 shorter events, 12.1 us)
Async XLA Ops:
  3.3 6.4 %copy-start.1 = (s32[1,32,8]{1,2,0:T(8,128)S(1)}, s32[1,32,8]{1,2,0:T(8,128)}, u32[]{:S(2)}) copy-start(s32[1,32,8]{1,2,0:T(8,128)} %param.9) | copy-start | bytes 3076
  3.3 53.6 %all-to-all-start = ((bf16[16,64,1024]{2,1,0:T(8,128)(2,1)}), bf16[16,64,1024]{2,1,0:T(8,128)(2,1)S(1)}, u32[]{:S(2)}, u32[]{:S(2)}) async-start(bf16[16,64,1024]{2,1,0:T(8,128)(2,1)} %broadcast_select_fusion), calls=%async_computation | async-start | bytes 4194304 | tf_op jit(solution)/shard_map/all_to_all | solution.py:46
  10.3 3.5 %copy-start = (bf16[1,256,1024]{2,1,0:T(8,128)(2,1)S(1)}, bf16[1,256,1024]{2,1,0:T(8,128)(2,1)}, u32[]{:S(2)}) copy-start(bf16[1,256,1024]{2,1,0:T(8,128)(2,1)} %param.7) | copy-start | bytes 1572868
  134.7 48.0 %collective-permute-start = (bf16[1,256,4096]{2,1,0:T(8,128)(2,1)}, bf16[1,256,4096]{2,1,0:T(8,128)(2,1)S(1)}, u32[]{:S(2)}, u32[]{:S(2)}) collective-permute-start(bf16[1,256,4096]{2,1,0:T(8,128)(2,1)} %reshape.41), channel_id=1, source_target_pairs={{0,16},{16,0},{1,17},{17,1},{2,18},{18,2},{3,19},{19,3},{4,20},{20... | collective-permute-start | bytes 6291464 | tf_op jit(solution)/shard_map/ppermute | solution.py:19
where the time goes:
time: 185 us; the launch traced here: 184 us
  waiting for transfers between devices  89.2 us (48%)
  local copies, waits for them, and re-layouts  41.6 us (22%)
  loops' own time  20.2 us (11%)
  matrix products  16 us (9%)
  other arithmetic  9.07 us (5%)
  starting transfers between devices  7.88 us (4%)
    ppermute x1, waiting for transfers between devices, from_behind(): lax.ppermute(x, axis, [(i, (i + by) % devices) for i in range(devices)])  46.5 us
    all_to_all x1, waiting for transfers between devices, on_device(): lax.all_to_all(outgoing, 'tok', split_axis=0, concat_axis=0, tiled=True)  42.7 us
    another operation x1, loops' own time, on_device(): results = lax.map(per_item, jnp.arange(QB_DEV * KV_HEADS))  20.2 us
    dot_general x8, matrix products, attend(): jnp.einsum('gqk,kd->qgd', weights, value_rows, preferred_element_type=jnp...  11.9 us
    dynamic_slice x16, local copies, waits for them, and re-layouts, per_item(): prefix_pairs[block_id, :, 1, head_id]  8.86 us
    dynamic_slice x8, local copies, waits for them, and re-layouts, per_item(): query_blocks[block_id, :, head_id]  7.81 us
    unnamed x8, local copies, waits for them, and re-layouts  6.54 us
    all_to_all x1, starting transfers between devices, on_device(): lax.all_to_all(outgoing, 'tok', split_axis=0, concat_axis=0, tiled=True)  6.37 us
  transfers between devices with their start and end apart: 2, of which 2 were waited for; matrix products, arithmetic and copies ran while one was open for 2% of the time, Pallas kernels for 0%

commit v1 on v0

v1 whole, which is shorter than its diff:
```python
import functools
import math

import jax
import jax.numpy as jnp
from jax import lax
from jax.experimental import pallas as pl
from jax.experimental.pallas import tpu as pltpu
from jax.sharding import PartitionSpec as P

HEAD = 128
BLOCK = 128
CORES = 2
MESH = pl.DeviceIdType.MESH
NEG = float("-inf")


def kernel(dims, served, q_hbm, suf_hbm, pre_hbm, out_hbm, *scratch):
    sections, far, near, kv_heads, depth, page, per_dev, group, unit = dims
    pages = scratch[:kv_heads]
    (q_v, suf_v, stage, keys, vals, q_sem, suf_sem, page_sem, s1, r1, s2, r2, s3, r3, s_out, r_out) = scratch[kv_heads:]
    tok = lax.axis_index("tok")
    sec = lax.axis_index("section")
    c = lax.rem(tok, CORES)
    b = lax.rem(tok // CORES, near)
    a = tok // (CORES * near)
    own = depth * page
    width = unit * HEAD
    units = group // unit

    def at(x, y, z):
        return {"tok": (x * near + y) * CORES + z}

    loads = []
    for h in range(kv_heads):
        for part in range(2):
            col = (part * kv_heads + h) * HEAD
            loads.append(
                pltpu.make_async_copy(
                    pre_hbm.at[0, 0, :, pl.ds(col, HEAD)], pages[h].at[c, b, a, part], page_sem.at[h, part]
                )
            )
    for load in loads:
        load.start()
    suf_load = pltpu.make_async_copy(suf_hbm.at[0], suf_v, suf_sem)
    suf_load.start()

    barrier = pltpu.get_barrier_semaphore()
    partners = [at(lax.rem(a + d, far), b, c) for d in range(1, far)]
    partners += [at(a, lax.rem(b + d, near), c) for d in range(1, near)]
    partners += [at(a, b, 1 - c)]
    ahead = {"section": lax.rem(sec + 1, sections)}
    partners += [ahead]
    if sections > 2:
        partners += [{"section": lax.rem(sec + sections - 1, sections)}]
    for partner in partners:
        pl.semaphore_signal(barrier, inc=1, device_id=partner, device_id_type=MESH)

    q_loads = {}
    for h in range(kv_heads):
        for blk in range(per_dev):
            where = (pl.ds(blk * BLOCK, BLOCK), pl.ds(h * group * HEAD, group * HEAD))
            q_loads[h, blk] = pltpu.make_async_copy(
                q_hbm.at[(0,) + where], q_v.at[where], q_sem.at[h, blk]
            )
            q_loads[h, blk].start()
    pl.semaphore_wait(barrier, len(partners))

    def remote(ref_src, ref_dst, send, recv, target):
        return pltpu.make_async_remote_copy(
            src_ref=ref_src, dst_ref=ref_dst, send_sem=send, recv_sem=recv, device_id=target, device_id_type=MESH
        )

    def first(h):
        return [
            remote(
                pages[h].at[c, b, a], pages[h].at[c, b, a], s1.at[h, d - 1], r1.at[h, d - 1],
                at(lax.rem(a + d, far), b, c),
            )
            for d in range(1, far)
        ]

    def second(h):
        return [
            remote(
                pages[h].at[c, b], pages[h].at[c, b], s2.at[h, d - 1], r2.at[h, d - 1],
                at(a, lax.rem(b + d, near), c),
            )
            for d in range(1, near)
        ]

    def third(h):
        return [remote(pages[h].at[c], pages[h].at[c], s3.at[h], r3.at[h], at(a, b, 1 - c))]

    def go(copies):
        for copy in copies:
            copy.start()

    def arrive(copies):
        for copy in copies:
            copy.wait_recv()

    def gone(copies):
        for copy in copies:
            copy.wait_send()

    def own_page(h):
        loads[2 * h].wait()
        loads[2 * h + 1].wait()

    def send_out(h, blk, u):
        where = (pl.ds(blk * BLOCK, BLOCK), pl.ds(pl.multiple_of((h * units + u) * width, width), width))
        index = (h * per_dev + blk) * units + u
        return remote(stage.at[where], out_hbm.at[(0,) + where], s_out.at[index], r_out.at[index], ahead)

    factor = math.log2(math.e) / math.sqrt(HEAD)
    causal = lax.broadcasted_iota(jnp.int32, (BLOCK, BLOCK), 1) <= lax.broadcasted_iota(
        jnp.int32, (BLOCK, BLOCK), 0
    )
    causal_bias = jnp.where(causal, 0.0, NEG).astype(jnp.float32)
    column = lax.broadcasted_iota(jnp.int32, (1, own), 1)

    def attend(h, blk):
        row = tok * per_dev + blk
        live = jnp.int32(0)
        for k in range(depth):
            pick = served[0, row, k]
            live = live + jnp.where(pick >= 0, 1, 0).astype(jnp.int32)
            pick = jnp.maximum(pick, 0)
            pc = lax.rem(pick, CORES)
            pb = lax.rem(lax.div(pick, CORES), near)
            pa = lax.div(pick, CORES * near)
            keys[pl.ds(k * page, page), :] = pages[h][pc, pb, pa, 0]
            vals[pl.ds(k * page, page), :] = pages[h][pc, pb, pa, 1]
        rows = pl.ds(blk * BLOCK, BLOCK)
        keys[pl.ds(own, BLOCK), :] = suf_v[rows, pl.ds(h * HEAD, HEAD)]
        vals[pl.ds(own, BLOCK), :] = suf_v[rows, pl.ds((kv_heads + h) * HEAD, HEAD)]
        bias = jnp.where(column < live * page, 0.0, NEG).astype(jnp.float32)
        q_loads[h, blk].wait()

        def step(u, carry):
            for j in range(unit):
                cols = pl.ds(pl.multiple_of(((h * units + u) * unit + j) * HEAD, HEAD), HEAD)
                scores = lax.dot_general(
                    q_v[rows, cols], keys[...], (((1,), (1,)), ((), ())), preferred_element_type=jnp.float32
                )
                left = scores[:, :own] + bias
                right = scores[:, own:] + causal_bias
                top = jnp.maximum(
                    jnp.max(left, axis=1, keepdims=True), jnp.max(right, axis=1, keepdims=True)
                )
                left = jnp.exp2((left - top) * factor)
                right = jnp.exp2((right - top) * factor)
                total = jnp.sum(left, axis=1, keepdims=True) + jnp.sum(right, axis=1, keepdims=True)
                weights = jnp.concatenate([left.astype(jnp.bfloat16), right.astype(jnp.bfloat16)], axis=1)
                mixed = jnp.dot(weights, vals[...], preferred_element_type=jnp.float32)
                stage[rows, cols] = (mixed / total).astype(jnp.bfloat16)
            send_out(h, blk, u).start()
            return carry

        lax.fori_loop(0, units, step, 0)

    p1 = [first(h) for h in range(kv_heads)]
    p2 = [second(h) for h in range(kv_heads)]
    p3 = [third(h) for h in range(kv_heads)]
    own_page(0)
    go(p1[0])
    arrive(p1[0])
    go(p2[0])
    own_page(1)
    go(p1[1])
    arrive(p2[0])
    go(p3[0])
    suf_load.wait()
    arrive(p3[0])
    for h in range(kv_heads):
        if h + 1 < kv_heads:
            arrive(p1[h + 1])
            go(p2[h + 1])
        if h + 2 < kv_heads:
            own_page(h + 2)
            go(p1[h + 2])
        for blk in range(per_dev):
            attend(h, blk)
            if blk == 0 and h + 1 < kv_heads:
                arrive(p2[h + 1])
                go(p3[h + 1])
        if h + 1 < kv_heads:
            arrive(p3[h + 1])
    for h in range(kv_heads):
        gone(p1[h])
        gone(p2[h])
        gone(p3[h])
    for h in range(kv_heads):
        for blk in range(per_dev):

            def finish(u, carry):
                copy = send_out(h, blk, u)
                copy.wait_send()
                copy.wait_recv()
                return carry

            lax.fori_loop(0, units, finish, 0)


def on_device(sections, toks, queries, suffix_kv, prefix_kv, served):
    rows, q_width = queries.shape[1:]
    kv_width = suffix_kv.shape[2]
    kv_heads = kv_width // (2 * HEAD)
    group = q_width // HEAD // kv_heads
    page = prefix_kv.shape[2]
    depth = served.shape[2]
    per_dev = rows // BLOCK
    chips = toks // CORES
    near = 1
    while 4 * near * near <= chips:
        near *= 2
    far = chips // near
    unit = 2
    dims = (sections, far, near, kv_heads, depth, page, per_dev, group, unit)
    keys = depth * page + BLOCK
    sends = kv_heads * group // unit * per_dev
    dma = pltpu.SemaphoreType.DMA
    any_ = pl.BlockSpec(memory_space=pl.ANY)
    bf16 = jnp.bfloat16
    return pl.pallas_call(
        functools.partial(kernel, dims),
        out_shape=jax.ShapeDtypeStruct(queries.shape, bf16),
        in_specs=[pl.BlockSpec(memory_space=pltpu.SMEM), any_, any_, any_],
        out_specs=any_,
        scratch_shapes=[pltpu.VMEM((CORES, near, far, 2, page, HEAD), bf16) for _ in range(kv_heads)]
        + [
            pltpu.VMEM((rows, q_width), bf16),
            pltpu.VMEM((rows, kv_width), bf16),
            pltpu.VMEM((rows, q_width), bf16),
            pltpu.VMEM((keys, HEAD), bf16),
            pltpu.VMEM((keys, HEAD), bf16),
            dma((kv_heads, per_dev)),
            dma,
            dma((kv_heads, 2)),
            dma((kv_heads, max(far - 1, 1))),
            dma((kv_heads, max(far - 1, 1))),
            dma((kv_heads, max(near - 1, 1))),
            dma((kv_heads, max(near - 1, 1))),
            dma((kv_heads,)),
            dma((kv_heads,)),
            dma((sends,)),
            dma((sends,)),
        ],
        compiler_params=pltpu.CompilerParams(
            collective_id=0, has_side_effects=True, vmem_limit_bytes=48 * 1024 * 1024
        ),
    )(served, queries, suffix_kv, prefix_kv)


def solution(mesh):
    placed = (
        P("section", "tok", None),
        P("section", "tok", None),
        P("section", "tok", None, None),
        P("section", None, None),
    )
    run = functools.partial(on_device, mesh.shape["section"], mesh.shape["tok"])
    return jax.shard_map(
        run, mesh=mesh, in_specs=placed, out_specs=P("section", "tok", None), check_vma=False
    )
```

time: 185 us -> 70.1 us (0.38)
  the two profiles are of different devices: /device:TPU:12 before, /device:TPU:0 now
where the time goes in v1:
time: 70.1 us; the launch traced here: 69.9 us
  Pallas kernels  64.2 us (92%)
  local copies, waits for them, and re-layouts  5.62 us (8%)
    pallas_call x1, Pallas kernels, on_device(): pl.pallas_call(functools.partial(kernel, dims), out_shape=jax.ShapeDtypeS...  64.2 us
    unnamed x8, local copies, waits for them, and re-layouts  5.62 us

profile of v1, /device:TPU:0, one launch (start us, length us, event | category | flops | bytes accessed | tf_op | source)
XLA Modules:
  0.0 69.9 jit_solution(7362327915282533624)
XLA Ops:
  0.0 0.8 %copy.5.served = s32[1,32,8]{2,1,0:T(8,128)S(1)} copy(s32[1,32,8]{1,2,0:T(8,128)} %param.7) | data formatting | bytes 2048 | tf_op args[3]
  0.8 0.0 copy-start
  0.8 1.6 %copy-done = bf16[1,256,4096]{2,1,0:T(8,128)(2,1)S(1)} copy-done((bf16[1,256,4096]{2,1,0:T(8,128)(2,1)S(1)}, bf16[1,256,4096]{2,1,0:T(8,128)(2,1)}, u32[]{:S(2)}) %copy-start) | copy-done | bytes 2097176
  2.4 0.0 copy-start.1
  2.4 1.0 %copy-done.1 = bf16[1,256,1024]{2,1,0:T(8,128)(2,1)S(1)} copy-done((bf16[1,256,1024]{2,1,0:T(8,128)(2,1)S(1)}, bf16[1,256,1024]{2,1,0:T(8,128)(2,1)}, u32[]{:S(2)}) %copy-start.1) | copy-done | bytes 524312
  3.4 0.0 copy-start.2
  3.4 0.9 %copy-done.2 = bf16[1,1,64,1024]{3,2,1,0:T(8,128)(2,1)S(1)} copy-done((bf16[1,1,64,1024]{3,2,1,0:T(8,128)(2,1)S(1)}, bf16[1,1,64,1024]{3,2,1,0:T(8,128)(2,1)}, u32[]{:S(2)}) %copy-start.2) | copy-done | bytes 131096
  4.3 64.2 %shard_map.46 = bf16[1,256,4096]{2,1,0:T(8,128)(2,1)S(1)} custom-call(s32[1,32,8]{2,1,0:T(8,128)S(1)} %copy.5.served, bf16[1,256,4096]{2,1,0:T(8,128)(2,1)S(1)} %copy-done, bf16[1,256,1024]{2,1,0:T(8,128)(2,1)S(1)} %copy-done.1, bf16[1,1,64,1024]{3,2,1,0:T(8,128)(2,1)S(1)} %copy-done.2), custom_call_target="tpu_custom_call" | custom-call | tf_op jit(solution)/shard_map/pallas_call | solution.py:226
  68.5 1.3 %copy.7 = bf16[1,256,4096]{2,1,0:T(8,128)(2,1)} copy(bf16[1,256,4096]{2,1,0:T(8,128)(2,1)S(1)} %shard_map.46) | data formatting | bytes 4194304
Async XLA Ops:
  0.8 1.6 %copy-start = (bf16[1,256,4096]{2,1,0:T(8,128)(2,1)S(1)}, bf16[1,256,4096]{2,1,0:T(8,128)(2,1)}, u32[]{:S(2)}) copy-start(bf16[1,256,4096]{2,1,0:T(8,128)(2,1)} %q_hbm.1) | copy-start | bytes 6291460
  2.4 1.0 %copy-start.1 = (bf16[1,256,1024]{2,1,0:T(8,128)(2,1)S(1)}, bf16[1,256,1024]{2,1,0:T(8,128)(2,1)}, u32[]{:S(2)}) copy-start(bf16[1,256,1024]{2,1,0:T(8,128)(2,1)} %suf_hbm.1) | copy-start | bytes 1572868
  3.4 0.9 %copy-start.2 = (bf16[1,1,64,1024]{3,2,1,0:T(8,128)(2,1)S(1)}, bf16[1,1,64,1024]{3,2,1,0:T(8,128)(2,1)}, u32[]{:S(2)}) copy-start(bf16[1,1,64,1024]{3,2,1,0:T(8,128)(2,1)} %pre_hbm.1) | copy-start | bytes 393220

commit v2 on v1

--- a/solution.py
+++ b/solution.py
@@ -15,10 +15,10 @@
 NEG = float("-inf")
 
 
-def kernel(dims, served, q_hbm, suf_hbm, pre_hbm, out_hbm, *scratch):
+def kernel(dims, served_hbm, q_hbm, suf_hbm, pre_hbm, out_hbm, *scratch):
     sections, far, near, kv_heads, depth, page, per_dev, group, unit = dims
     pages = scratch[:kv_heads]
-    (q_v, suf_v, stage, keys, vals, q_sem, suf_sem, page_sem, s1, r1, s2, r2, s3, r3, s_out, r_out) = scratch[kv_heads:]
+    (served, served_sem, q_v, suf_v, stage, keys, vals, q_sem, suf_sem, page_sem, s1, r1, s2, r2, s3, r3, s_out, r_out) = scratch[kv_heads:]
     tok = lax.axis_index("tok")
     sec = lax.axis_index("section")
     c = lax.rem(tok, CORES)
@@ -31,6 +31,8 @@
     def at(x, y, z):
         return {"tok": (x * near + y) * CORES + z}
 
+    served_load = pltpu.make_async_copy(served_hbm, served, served_sem)
+    served_load.start()
     loads = []
     for h in range(kv_heads):
         for part in range(2):
@@ -172,6 +174,7 @@
     arrive(p2[0])
     go(p3[0])
     suf_load.wait()
+    served_load.wait()
     arrive(p3[0])
     for h in range(kv_heads):
         if h + 1 < kv_heads:
@@ -226,10 +229,12 @@
     return pl.pallas_call(
         functools.partial(kernel, dims),
         out_shape=jax.ShapeDtypeStruct(queries.shape, bf16),
-        in_specs=[pl.BlockSpec(memory_space=pltpu.SMEM), any_, any_, any_],
+        in_specs=[pl.BlockSpec(memory_space=pltpu.HBM)] * 4,
         out_specs=any_,
         scratch_shapes=[pltpu.VMEM((CORES, near, far, 2, page, HEAD), bf16) for _ in range(kv_heads)]
         + [
+            pltpu.SMEM(served.shape, served.dtype),
+            dma,
             pltpu.VMEM((rows, q_width), bf16),
             pltpu.VMEM((rows, kv_width), bf16),
             pltpu.VMEM((rows, q_width), bf16),
@@ -248,7 +253,7 @@
             dma((sends,)),
         ],
         compiler_params=pltpu.CompilerParams(
-            collective_id=0, has_side_effects=True, vmem_limit_bytes=48 * 1024 * 1024
+            collective_id=0, has_side_effects=True, vmem_limit_bytes=61 * 1024 * 1024
         ),
     )(served, queries, suffix_kv, prefix_kv)
 

time: 70.1 us -> 68.1 us (0.971)
  local copies, waits for them, and re-layouts: 5.62 us -> 4.49 us
  Pallas kernels: 64.2 us -> 63.4 us
    unnamed x8 -> x2, local copies, waits for them, and re-layouts: 5.62 us -> 4.49 us
    pallas_call x1, Pallas kernels: 64.2 us -> 63.4 us  [on_device(): pl.pallas_call(functools.partial(kernel, dims), out_shape=jax.ShapeDtypeS...]
where the time goes in v2:
time: 68.1 us; the launch traced here: 67.9 us
  Pallas kernels  63.4 us (93%)
  local copies, waits for them, and re-layouts  4.49 us (7%)
    pallas_call x1, Pallas kernels, on_device(): pl.pallas_call(functools.partial(kernel, dims), out_shape=jax.ShapeDtypeS...  63.4 us
    unnamed x2, local copies, waits for them, and re-layouts  4.49 us

profile of v2, /device:TPU:0, one launch (start us, length us, event | category | flops | bytes accessed | tf_op | source)
XLA Modules:
  0.0 67.9 jit_solution(17817178885003598234)
XLA Ops:
  0.0 1.4 %copy.5.served_hbm = s32[1,32,8]{2,1,0:T(8,128)} copy(s32[1,32,8]{1,2,0:T(8,128)} %param.7) | data formatting | bytes 2048 | tf_op args[3]
  1.4 63.4 %shard_map.46 = bf16[1,256,4096]{2,1,0:T(8,128)(2,1)} custom-call(s32[1,32,8]{2,1,0:T(8,128)} %copy.5.served_hbm, bf16[1,256,4096]{2,1,0:T(8,128)(2,1)} %q_hbm.1, bf16[1,256,1024]{2,1,0:T(8,128)(2,1)} %suf_hbm.1, bf16[1,1,64,1024]{3,2,1,0:T(8,128)(2,1)} %pre_hbm.1), custom_call_target="tpu_custom_call" | custom-call | tf_op jit(solution)/shard_map/pallas_call | solution.py:229
  64.8 3.1 %copy.7 = bf16[1,256,4096]{2,1,0:T(8,128)(2,1)} copy(bf16[1,256,4096]{2,1,0:T(8,128)(2,1)} %shard_map.46) | data formatting | bytes 4194304
